TPU v7x, 32 devices: a whole 2x2x4 slice. The times are simulated.
32 devices in a mesh: dp: 8 (over z, y), ep: 4 (over x, core).
Axes of the slice: x: 2, y: 2, z: 4, core: 2. Of those that a mesh axis runs over, the one named last changes fastest.
Arguments:
- grad: float32 [2, 1536, 3584], P(None, 'dp', 'ep'), may hold values from -40 to 40
- momentum: float32 [2, 1536, 3584], P(None, 'dp', 'ep'), may hold values from -6 to 6
- lengths: int32 [2, 8], replicated, may hold values from 1 to 192, 1024 in all within a row
Outputs:
- new_momentum: float32 [2, 1536, 3584], P(None, 'dp', 'ep')
- update: float32 [2, 1536, 3584], P(None, 'dp', 'ep')
Inputs may be any that keep to these rules, and one draw needn't show every extreme that they name: lengths[j, d] counts the rows of matrix j held by dp index d, in order of d, in the first slots of its block of 192 slots; each row of lengths sums to 1024 and reaches 192.
All inputs are finite; a program needn't handle non-finite values.
Results may differ from a plain program's by a relative error of at most 0.009.
Values may be sent and summed in bfloat16 or wider, within the bound.
A program may use at most 64 MiB of HBM per device.

v0:
```python
import math

import jax
import jax.numpy as jnp
from jax import lax
from jax.sharding import PartitionSpec as P

H = 1024
D = 3584


MOMENTUM_COEF = 0.95
EPSILON = 1e-06
FIRST_LIN = 3.0
FIRST_CUBE = -2.5
SECOND_LIN = 1.5
SECOND_CUBE = -0.5


def from_root(block, axis, owner):
    block = jnp.where(lax.axis_index(axis) == owner, block, jnp.zeros_like(block))
    return lax.psum(block, axis)


def newton_polar(scaled_gram, factor, matrix):
    product = jnp.dot(scaled_gram, matrix, preferred_element_type=jnp.float32)
    first_iter = (factor * (FIRST_LIN * matrix.astype(jnp.float32) + FIRST_CUBE * product)).astype(
        jnp.bfloat16
    )
    product = jnp.dot(scaled_gram, first_iter, preferred_element_type=jnp.float32)
    applied = (FIRST_LIN * first_iter.astype(jnp.float32) + FIRST_CUBE * product).astype(
        jnp.bfloat16
    )
    second = jnp.dot(scaled_gram, applied, preferred_element_type=jnp.float32).astype(jnp.bfloat16)
    third = FIRST_LIN * second.astype(jnp.float32) + FIRST_CUBE * jnp.dot(
        scaled_gram, second, preferred_element_type=jnp.float32
    )
    return (SECOND_LIN * first_iter.astype(jnp.float32) + SECOND_CUBE * third).astype(jnp.bfloat16)


def body(grad, momentum, lengths):
    matrices = grad.shape[0]
    slot_rows = grad.shape[1]
    columns = grad.shape[2]
    new_momentum = MOMENTUM_COEF * momentum + grad
    rounded = (grad + MOMENTUM_COEF * new_momentum).astype(jnp.bfloat16)
    holders = lax.axis_size("dp")
    myself = lax.axis_index("dp")
    is_owner = myself < matrices
    chosen = jnp.minimum(myself, matrices - 1)
    offsets = jnp.cumsum(lengths, axis=1) - lengths
    chosen_len = lax.dynamic_index_in_dim(lengths, chosen, 0, keepdims=False)
    chosen_off = lax.dynamic_index_in_dim(offsets, chosen, 0, keepdims=False)
    device_ids = jnp.arange(holders, dtype=jnp.int32)
    portion = lax.all_gather(rounded, "dp", axis=1, tiled=True)
    piece_rows = portion.shape[1]
    incoming = lax.dynamic_index_in_dim(portion, chosen, 0, keepdims=False)
    slot_ids = jnp.arange(piece_rows, dtype=jnp.int32)
    source = slot_ids // slot_rows
    within = slot_ids % slot_rows
    matches = source[:, None] == device_ids[None, :]
    length_at = jnp.sum(jnp.where(matches, chosen_len[None, :], 0), axis=1)
    offset_at = jnp.sum(jnp.where(matches, chosen_off[None, :], 0), axis=1)
    keep = jnp.logical_and(within < length_at, is_owner)
    target = jnp.where(keep, offset_at + within, H)
    matrix = jnp.zeros((H, columns), jnp.bfloat16).at[target].set(incoming, mode="drop")
    portion = lax.all_gather(matrix, "ep", axis=1, tiled=True)
    gram_full = jnp.dot(portion, portion.T, preferred_element_type=jnp.float32)
    scale_sq = lax.rsqrt(jnp.sum(gram_full * gram_full) + EPSILON)
    scaled_gram = (scale_sq * gram_full).astype(jnp.bfloat16)
    ortho = newton_polar(scaled_gram, jnp.sqrt(scale_sq), matrix)
    scale_out = math.sqrt(max(H, D))
    positions = jnp.arange(slot_rows, dtype=jnp.int32)
    results = []
    for matrix_id in range(matrices):
        owned_ortho = from_root(ortho, "dp", matrix_id)
        own_length = lax.dynamic_index_in_dim(lengths[matrix_id], myself, 0, keepdims=False)
        own_offset = lax.dynamic_index_in_dim(offsets[matrix_id], myself, 0, keepdims=False)
        is_valid = positions < own_length
        picked = jnp.take(owned_ortho, jnp.where(is_valid, own_offset + positions, 0), axis=0)
        results.append(
            jnp.where(is_valid[:, None], picked.astype(jnp.float32) * scale_out, jnp.float32(0.0))
        )
    return (new_momentum, jnp.stack(results))


def solution(mesh):
    return jax.shard_map(
        body,
        mesh=mesh,
        in_specs=(P(None, "dp", "ep"), P(None, "dp", "ep"), P()),
        out_specs=(P(None, "dp", "ep"), P(None, "dp", "ep")),
        check_vma=False,
    )
```

profile of v0, /device:TPU:0, one launch (start us, length us, event | category | flops | bytes accessed | tf_op | source)
XLA Modules:
  0.0 356.7 jit_solution(17956882732598681466)
XLA Ops:
  7.2 0.0 copy-start.2
  7.2 0.0 all-gather.3.cloned.1.call-start
  7.2 3.3 add_convert_fusion
  10.5 0.0 all-gather.3.cloned.1.call-update
  10.5 0.0 all-gather.5.cloned.1.call-start
  10.6 0.0 copy-done.2
  10.6 0.2 reduce_window_sum.11
  10.8 0.1 select_reduce_fusion.1
  10.9 0.1 fusion.12
  11.0 92.0 %all-gather.3.cloned.1.call-done = bf16[2,1536,896]{2,1,0:T(8,128)(2,1)} async-done(((bf16[2,192,896]{2,1,0:T(8,128)(2,1)}), bf16[2,1536,896]{2,1,0:T(8,128)(2,1)}) %all-gather.3.cloned.1.call-update) | async-done | bytes 5505040 | tf_op jit(solution)/shard_map/all_gather | solution.py:55
  103.0 9.6 %scatter_custom_fusion = bf16[1024,896]{1,0:T(8,128)(2,1)} fusion(s32[1536]{0:T(1024)S(1)} %fusion.12, bf16[2,1536,896]{2,1,0:T(8,128)(2,1)} %all-gather.3.cloned.1.call-done, s32[]{:T(128)S(6)} %select_n.108, s32[]{:T(128)} %constant.73.clone.1, bf16[]{:T(256)} %constant.77.clone.1), kind=kCustom, calls=%fused_computation.12 | custom fusion | bytes 4588548 | tf_op jit(solution)/shard_map/scatter | solution.py:66
  112.5 0.0 all-gather.5.cloned.1.call-update
  112.6 0.2 all-reduce.3.cloned.1.call-start
  112.8 50.4 %all-gather.5.cloned.1.call-done = bf16[1024,3584]{1,0:T(8,128)(2,1)} async-done(((bf16[1024,896]{1,0:T(8,128)(2,1)}), bf16[1024,3584]{1,0:T(8,128)(2,1)}) %all-gather.5.cloned.1.call-update) | async-done | bytes 7340048 | tf_op jit(solution)/shard_map/all_gather | solution.py:67
  163.2 15.1 %multiply_reduce_fusion = (f32[]{:T(128)}, f32[1024,1024]{1,0:T(8,128)}) fusion(bf16[1024,3584]{1,0:T(8,128)(2,1)} %all-gather.5.cloned.1.call-done), kind=kOutput, calls=%fused_computation.6 | convolution fusion | flops 7518289920 | bytes 11534340 | tf_op jit(solution)/shard_map/dot_general | solution.py:68
  179.0 0.0 copy-start
  179.0 2.9 multiply_convert_fusion
  181.9 0.0 copy-done
  181.9 3.6 %multiply_convert_fusion.1 = bf16[1024,896]{1,0:T(8,128)(2,1)} fusion(bf16[1024,896]{1,0:T(8,128)(2,1)S(1)} %copy-done, bf16[1024,1024]{1,0:T(8,128)(2,1)S(1)} %multiply_convert_fusion, f32[]{:T(128)S(6)} %sqrt.3), kind=kOutput, calls=%fused_computation.11 | convolution fusion | flops 1884553216 | bytes 5767172 | tf_op jit(solution)/shard_map/dot_general | solution.py:26
  185.6 7.8 %fusion.9 = bf16[1024,896]{1,0:T(8,128)(2,1)} fusion(bf16[1024,1024]{1,0:T(8,128)(2,1)S(1)} %multiply_convert_fusion, bf16[1024,896]{1,0:T(8,128)(2,1)} %multiply_convert_fusion.1), kind=kOutput, calls=%fused_computation.22 | convolution fusion | flops 3762683904 | bytes 5767168 | tf_op jit(solution)/shard_map/dot_general | solution.py:34
  193.4 7.4 %broadcast_select_fusion.1 = (bf16[1024,896]{1,0:T(8,128)(2,1)}, bf16[1024,896]{1,0:T(8,128)(2,1)}) fusion(pred[]{:T(512)S(6)} %eq.27, pred[]{:T(512)S(6)} %eq.31, bf16[1024,1024]{1,0:T(8,128)(2,1)S(1)} %multiply_convert_fusion, bf16[1024,896]{1,0:T(8,128)(2,1)} %fusion.9, bf16[1024,896]{1,0:T(8,128)(2,1)} %multiply_convert_fusion.1), kind=kOutput, calls=%fused_computation.17 | convolution fusion | flops 1889140736 | bytes 9437186 | tf_op jit(solution)/shard_map/dot_general | solution.py:35
  200.7 0.0 all-reduce.3.cloned.1.call-update
  200.8 0.6 constant_dynamic-slice_fusion.5
  201.4 0.6 constant_dynamic-slice_fusion
  202.0 0.6 constant_dynamic-slice_fusion.1
  202.7 0.6 constant_dynamic-slice_fusion.4
  203.3 0.6 iota_compare_fusion.2
  203.9 0.7 iota_compare_fusion.1
  204.6 2.6 compare_and_fusion
  207.2 2.6 compare_select_fusion.1
  209.8 134.6 %all-reduce.3.cloned.1.call-done = (bf16[1024,896]{1,0:T(8,128)(2,1)}, bf16[1024,896]{1,0:T(8,128)(2,1)}) async-done(((bf16[1024,896]{1,0:T(8,128)(2,1)}, bf16[1024,896]{1,0:T(8,128)(2,1)}), (bf16[1024,896]{1,0:T(8,128)(2,1)}, bf16[1024,896]{1,0:T(8,128)(2,1)})) %all-reduce.3.cloned.1.call-update) | async-done | bytes 3670032 | tf_op jit(solution)/shard_map/psum | solution.py:22
  344.4 0.0 copy-start.1
  344.4 3.1 gather_fusion
  347.6 0.0 copy-done.1
  347.6 1.0 gather_fusion.1
  348.6 0.2 select_bitcast_fusion.1
  348.8 0.2 select_bitcast_fusion
  349.0 1.2 pad_maximum_fusion
  (6 shorter events, 0.0 us)
Async XLA Ops:
  7.2 3.4 copy-start.2
  7.2 95.8 %all-gather.3.cloned.1.call-start = ((), (), s32[]{:S(2)}) async-start(), calls=%async_computation | async-start | bytes 6193152 | tf_op jit(solution)/shard_map/all_gather | solution.py:55
  10.5 152.6 %all-gather.5.cloned.1.call-start = ((), (), s32[]{:S(2)}) async-start(), calls=%async_computation.1 | async-start | bytes 9175040 | tf_op jit(solution)/shard_map/all_gather | solution.py:67
  112.6 231.9 %all-reduce.3.cloned.1.call-start = ((), (), s32[]{:S(2)}) async-start(), calls=%async_computation.2 | async-start | bytes 7340032 | tf_op jit(solution)/shard_map/psum | solution.py:22
  179.0 2.9 copy-start
  344.4 3.1 copy-start.1
Sparse Core Ops, SparseCore 0:
  10.8 92.1 all-gather.2
  112.7 50.4 all-gather.4
  200.9 143.4 all-reduce.2
where the time goes:
time: 357 us
  waiting for transfers between devices  277 us (78%)
  matrix products  33.9 us (9%)
  local copies, waits for them, and re-layouts  16.3 us (5%)
  other arithmetic  14.6 us (4%)
  between operations  14.6 us (4%)
    psum x1, waiting for transfers between devices, from_root(): return lax.psum(block, axis)  135 us
    all_gather x1, waiting for transfers between devices, body(): portion = lax.all_gather(rounded, 'dp', axis=1, tiled=True)  92 us
    all_gather x1, waiting for transfers between devices, body(): portion = lax.all_gather(matrix, 'ep', axis=1, tiled=True)  50.4 us
    dot_general x1, matrix products, body(): gram_full = jnp.dot(portion, portion.T, preferred_element_type=jnp.float32)  15.1 us
    scatter x1, local copies, waits for them, and re-layouts, body(): jnp.zeros((H, columns), jnp.bfloat16).at[target].set(incoming, mode='drop')  9.57 us
    dot_general x1, matrix products, newton_polar(): jnp.dot(scaled_gram, applied, preferred_element_type=jnp.float32)  7.79 us
    dot_general x1, matrix products, newton_polar(): jnp.dot(scaled_gram, second, preferred_element_type=jnp.float32)  7.39 us
  transfers between devices with their start and end apart: 3, of which 3 were waited for; matrix products, arithmetic and copies ran while one was open for 3% of the time, Pallas kernels for 0%

commit v1 on v0

--- a/solution.py
+++ b/solution.py
@@ -1,8 +1,11 @@
+import functools
 import math
 
 import jax
 import jax.numpy as jnp
 from jax import lax
+from jax.experimental import pallas as pl
+from jax.experimental.pallas import tpu as pltpu
 from jax.sharding import PartitionSpec as P
 
 H = 1024
@@ -15,6 +18,12 @@
 FIRST_CUBE = -2.5
 SECOND_LIN = 1.5
 SECOND_CUBE = -0.5
+
+LANES = 128
+BLOCKS = 8
+KEPT = BLOCKS // 2 + 1
+MESH = pl.DeviceIdType.MESH
+VMEM_LIMIT = 48 * 1024 * 1024
 
 
 def from_root(block, axis, owner):
@@ -38,7 +47,7 @@
     return (SECOND_LIN * first_iter.astype(jnp.float32) + SECOND_CUBE * third).astype(jnp.bfloat16)
 
 
-def body(grad, momentum, lengths):
+def gathered_body(grad, momentum, lengths):
     matrices = grad.shape[0]
     slot_rows = grad.shape[1]
     columns = grad.shape[2]
@@ -84,11 +93,411 @@
     return (new_momentum, jnp.stack(results))
 
 
+def far_first(count):
+    return sorted(range(1, count), key=lambda r: abs(r - count // 2))
+
+
+def meet(partners):
+    barrier = pltpu.get_barrier_semaphore()
+    for partner in partners:
+        pl.semaphore_signal(barrier, inc=1, device_id=partner, device_id_type=MESH)
+    pl.semaphore_wait(barrier, len(partners))
+
+
+def other_core(ep):
+    return ep + 1 - 2 * lax.rem(ep, 2)
+
+
+def spread_kernel(holders, send_ref, held_ref, sent, landed, passed, got, local):
+    me, ep = lax.axis_index("dp"), lax.axis_index("ep")
+    sibling = (me, other_core(ep))
+    meet([(lax.rem(me + r, holders), ep) for r in range(1, holders)] + [sibling])
+
+    copies = {}
+    for r in far_first(holders):
+        to = lax.rem(me + r, holders)
+        copies[r] = pltpu.make_async_remote_copy(
+            src_ref=send_ref.at[to],
+            dst_ref=held_ref.at[0, me],
+            send_sem=sent.at[r],
+            recv_sem=landed.at[r],
+            device_id=(to, ep),
+            device_id_type=MESH,
+        )
+        copies[r].start()
+    own = pltpu.make_async_copy(send_ref.at[me], held_ref.at[0, me], local)
+    own.start()
+    forwards = [
+        pltpu.make_async_remote_copy(
+            src_ref=send_ref.at[me],
+            dst_ref=held_ref.at[1, me],
+            send_sem=passed.at[0],
+            recv_sem=got.at[0],
+            device_id=sibling,
+            device_id_type=MESH,
+        )
+    ]
+    forwards[0].start()
+    for r in reversed(far_first(holders)):
+        source = lax.rem(me + holders - r, holders)
+        copies[r].wait_recv()
+        forward = pltpu.make_async_remote_copy(
+            src_ref=held_ref.at[0, source],
+            dst_ref=held_ref.at[1, source],
+            send_sem=passed.at[r],
+            recv_sem=got.at[r],
+            device_id=sibling,
+            device_id_type=MESH,
+        )
+        forward.start()
+        forwards.append(forward)
+    own.wait()
+    for r in far_first(holders):
+        copies[r].wait_send()
+    for forward in forwards:
+        forward.wait()
+
+
+def spread(chunks):
+    holders = chunks.shape[0]
+    dma = pltpu.SemaphoreType.DMA
+    return pl.pallas_call(
+        functools.partial(spread_kernel, holders),
+        out_shape=jax.ShapeDtypeStruct((2,) + chunks.shape, chunks.dtype),
+        in_specs=[pl.BlockSpec(memory_space=pl.ANY)],
+        out_specs=pl.BlockSpec(memory_space=pl.ANY),
+        scratch_shapes=[dma((holders,)), dma((holders,)), dma((holders,)), dma((holders,)), dma],
+        compiler_params=pltpu.CompilerParams(collective_id=0, has_side_effects=True),
+        name="spread",
+    )(chunks)
+
+
+def collect_kernel(holders, send_ref, held_ref, sent, landed, local):
+    me, ep = lax.axis_index("dp"), lax.axis_index("ep")
+    meet([(lax.rem(me + r, holders), ep) for r in range(1, holders)])
+    copies = []
+    for r in far_first(holders):
+        to = lax.rem(me + r, holders)
+        copy = pltpu.make_async_remote_copy(
+            src_ref=send_ref.at[to],
+            dst_ref=held_ref.at[me],
+            send_sem=sent.at[r],
+            recv_sem=landed.at[r],
+            device_id=(to, ep),
+            device_id_type=MESH,
+        )
+        copy.start()
+        copies.append(copy)
+    own = pltpu.make_async_copy(send_ref.at[me], held_ref.at[me], local)
+    own.start()
+    own.wait()
+    for copy in copies:
+        copy.wait()
+
+
+def collect(chunks):
+    holders = chunks.shape[0]
+    dma = pltpu.SemaphoreType.DMA
+    return pl.pallas_call(
+        functools.partial(collect_kernel, holders),
+        out_shape=jax.ShapeDtypeStruct(chunks.shape, chunks.dtype),
+        in_specs=[pl.BlockSpec(memory_space=pl.ANY)],
+        out_specs=pl.BlockSpec(memory_space=pl.ANY),
+        scratch_shapes=[dma((holders,)), dma((holders,)), dma],
+        compiler_params=pltpu.CompilerParams(collective_id=1, has_side_effects=True),
+        name="collect",
+    )(chunks)
+
+
+def reduce_kernel(
+    group, peers, parts_ref, whole_ref, terms, reduced, sent, landed, out, into, passed, got, local
+):
+    dp, ep = lax.axis_index("dp"), lax.axis_index("ep")
+    chips = peers // group
+    base, core = dp - lax.rem(dp, group), lax.rem(ep, 2)
+    me = lax.rem(dp, group) * chips + ep // 2
+    sibling = (dp, other_core(ep))
+
+    def device(index):
+        return (base + index // chips, lax.rem(index, chips) * 2 + core)
+
+    meet([device(lax.rem(me + r, peers)) for r in range(1, peers)] + [sibling])
+
+    copies = []
+    for r in range(1, peers):
+        to = lax.rem(me + r, peers)
+        copy = pltpu.make_async_remote_copy(
+            src_ref=parts_ref.at[to],
+            dst_ref=terms.at[r],
+            send_sem=sent.at[r],
+            recv_sem=landed.at[r],
+            device_id=device(to),
+            device_id_type=MESH,
+        )
+        copy.start()
+        copies.append(copy)
+    total = parts_ref[me].astype(jnp.float32)
+    for r in range(1, peers):
+        copies[r - 1].wait_recv()
+        total = total + terms[r].astype(jnp.float32)
+    reduced[...] = total.astype(reduced.dtype)
+
+    spreads = []
+    for r in range(1, peers):
+        copy = pltpu.make_async_remote_copy(
+            src_ref=reduced,
+            dst_ref=whole_ref.at[0, me],
+            send_sem=out.at[r],
+            recv_sem=into.at[r],
+            device_id=device(lax.rem(me + r, peers)),
+            device_id_type=MESH,
+        )
+        copy.start()
+        spreads.append(copy)
+    own = pltpu.make_async_copy(reduced, whole_ref.at[0, me], local)
+    own.start()
+    forwards = [
+        pltpu.make_async_remote_copy(
+            src_ref=reduced,
+            dst_ref=whole_ref.at[1, me],
+            send_sem=passed.at[0],
+            recv_sem=got.at[0],
+            device_id=sibling,
+            device_id_type=MESH,
+        )
+    ]
+    forwards[0].start()
+    for r in range(1, peers):
+        source = lax.rem(me + peers - r, peers)
+        spreads[r - 1].wait_recv()
+        forward = pltpu.make_async_remote_copy(
+            src_ref=whole_ref.at[0, source],
+            dst_ref=whole_ref.at[1, source],
+            send_sem=passed.at[r],
+            recv_sem=got.at[r],
+            device_id=sibling,
+            device_id_type=MESH,
+        )
+        forward.start()
+        forwards.append(forward)
+    own.wait()
+    for copy in copies:
+        copy.wait_send()
+    for copy in spreads:
+        copy.wait_send()
+    for forward in forwards:
+        forward.wait()
+
+
+def reduce_parts(parts, group):
+    peers = parts.shape[0]
+    dma = pltpu.SemaphoreType.DMA
+    return pl.pallas_call(
+        functools.partial(reduce_kernel, group, peers),
+        out_shape=jax.ShapeDtypeStruct((2,) + parts.shape, parts.dtype),
+        in_specs=[pl.BlockSpec(memory_space=pltpu.VMEM)],
+        out_specs=pl.BlockSpec(memory_space=pl.ANY),
+        scratch_shapes=[
+            pltpu.VMEM(parts.shape, parts.dtype),
+            pltpu.VMEM(parts.shape[1:], parts.dtype),
+        ]
+        + [dma((peers,))] * 6
+        + [dma],
+        compiler_params=pltpu.CompilerParams(
+            collective_id=2, has_side_effects=True, vmem_limit_bytes=VMEM_LIMIT
+        ),
+        name="reduce_parts",
+    )(parts)
+
+
+def gram_kernel(target_ref, held_ref, matrix_ref, parts_ref, both):
+    height, width = matrix_ref.shape
+    slots = held_ref.shape[1]
+    tile = 256
+    target = target_ref[...]
+
+    def pack(step, carry):
+        start = pl.multiple_of(step * tile, tile)
+        rows = lax.broadcasted_iota(jnp.int32, (tile, slots), 0) + start
+        chosen = jnp.where(rows == target, 1.0, 0.0).astype(jnp.bfloat16)
+        mine = jnp.dot(chosen, held_ref[0], preferred_element_type=jnp.float32)
+        mine = mine.astype(jnp.bfloat16)
+        matrix_ref[pl.ds(start, tile), :] = mine
+        both[pl.ds(start, tile), :width] = mine
+        theirs = jnp.dot(chosen, held_ref[1], preferred_element_type=jnp.float32)
+        both[pl.ds(start, tile), width:] = theirs.astype(jnp.bfloat16)
+        return carry
+
+    lax.fori_loop(0, height // tile, pack, 0)
+    block = height // BLOCKS
+
+    def multiply(step, carry):
+        start = pl.multiple_of(step * block, block)
+        part = lax.dot_general(
+            both[pl.ds(start, block), :],
+            both[pl.ds(start, KEPT * block), :],
+            (((1,), (1,)), ((), ())),
+            preferred_element_type=jnp.float32,
+        )
+        parts_ref[pl.ds(start, block), :] = part.astype(jnp.bfloat16)
+        return carry
+
+    lax.fori_loop(0, BLOCKS // 2, multiply, 0)
+
+
+def local_gram(target, held):
+    width = held.shape[2]
+    return pl.pallas_call(
+        gram_kernel,
+        out_shape=(
+            jax.ShapeDtypeStruct((H, width), jnp.bfloat16),
+            jax.ShapeDtypeStruct((H // 2, KEPT * (H // BLOCKS)), jnp.bfloat16),
+        ),
+        scratch_shapes=[pltpu.VMEM((H, 2 * width), jnp.bfloat16)],
+        compiler_params=pltpu.CompilerParams(vmem_limit_bytes=VMEM_LIMIT),
+        name="local_gram",
+    )(target, held)
+
+
+def chain_kernel(slot_rows, target_ref, blocks_ref, matrix_ref, slots_ref, gram, first, applied):
+    height, width = matrix_ref.shape
+    block = height // BLOCKS
+    squares = jnp.zeros((8, LANES), jnp.float32)
+    for i in range(BLOCKS):
+        for k in range(KEPT):
+            piece = blocks_ref[pl.ds(i * block, block), pl.ds(k * block, block)]
+            j = (i + k) % BLOCKS
+            gram[pl.ds(i * block, block), pl.ds(j * block, block)] = piece
+            wide = piece.astype(jnp.float32)
+            if 0 < k < BLOCKS - KEPT + 1:
+                gram[pl.ds(j * block, block), pl.ds(i * block, block)] = wide.T.astype(jnp.bfloat16)
+            weight = 2.0 if 0 < k < BLOCKS - KEPT + 1 else 1.0
+            square = (wide * wide).reshape(-1, 8, block).sum(axis=0)
+            for lane in range(block // LANES):
+                squares = squares + weight * square[:, lane * LANES : (lane + 1) * LANES]
+    scale_sq = lax.rsqrt(jnp.sum(squares, keepdims=True) + EPSILON)
+    factor = jnp.sqrt(scale_sq)
+    tile = 256
+    steps = height // tile
+
+    def product(start, right):
+        return scale_sq * jnp.dot(
+            gram[pl.ds(start, tile), :], right[...], preferred_element_type=jnp.float32
+        )
+
+    def each(step):
+        def run(index, carry):
+            step(pl.multiple_of(index * tile, tile))
+            return carry
+
+        lax.fori_loop(0, steps, run, 0)
+
+    def one(start):
+        rows = matrix_ref[pl.ds(start, tile), :].astype(jnp.float32)
+        value = factor * (FIRST_LIN * rows + FIRST_CUBE * product(start, matrix_ref))
+        first[pl.ds(start, tile), :] = value.astype(jnp.bfloat16)
+
+    def two(start):
+        rows = first[pl.ds(start, tile), :].astype(jnp.float32)
+        value = FIRST_LIN * rows + FIRST_CUBE * product(start, first)
+        applied[0, pl.ds(start, tile), :] = value.astype(jnp.bfloat16)
+
+    def three(start):
+        value = product(start, applied.at[0])
+        applied[1, pl.ds(start, tile), :] = value.astype(jnp.bfloat16)
+
+    def four(start):
+        rows = applied[1, pl.ds(start, tile), :].astype(jnp.float32)
+        third = FIRST_LIN * rows + FIRST_CUBE * product(start, applied.at[1])
+        rows = first[pl.ds(start, tile), :].astype(jnp.float32)
+        value = SECOND_LIN * rows + SECOND_CUBE * third
+        applied[0, pl.ds(start, tile), :] = value.astype(jnp.bfloat16)
+
+    for step in (one, two, three, four):
+        each(step)
+
+    def lay_out(index, carry):
+        start = pl.multiple_of(index * slot_rows, slot_rows)
+        wanted = lax.broadcasted_iota(jnp.int32, (slot_rows, height), 1)
+        chosen = jnp.where(wanted == target_ref[pl.ds(start, slot_rows), :], 1.0, 0.0)
+        rows = jnp.dot(
+            chosen.astype(jnp.bfloat16), applied[0], preferred_element_type=jnp.float32
+        )
+        slots_ref[pl.ds(start, slot_rows), :] = rows.astype(jnp.bfloat16)
+        return carry
+
+    lax.fori_loop(0, slots_ref.shape[0] // slot_rows, lay_out, 0)
+
+
+def apply_chain(target, blocks, matrix, slot_rows):
+    width = matrix.shape[1]
+    return pl.pallas_call(
+        functools.partial(chain_kernel, slot_rows),
+        out_shape=jax.ShapeDtypeStruct((target.shape[0], width), jnp.bfloat16),
+        scratch_shapes=[
+            pltpu.VMEM((H, H), jnp.bfloat16),
+            pltpu.VMEM((H, width), jnp.bfloat16),
+            pltpu.VMEM((2, H, width), jnp.bfloat16),
+        ],
+        compiler_params=pltpu.CompilerParams(vmem_limit_bytes=VMEM_LIMIT),
+        name="apply_chain",
+    )(target, blocks, matrix)
+
+
+def chunk_width(columns, group):
+    return -(-columns // (group * LANES)) * LANES
+
+
+def split_body(grad, momentum, lengths):
+    matrices, slot_rows, columns = grad.shape
+    holders = lax.axis_size("dp")
+    group = holders // matrices
+    width = chunk_width(columns, group)
+    peers = group * (lax.axis_size("ep") // 2)
+    new_momentum = MOMENTUM_COEF * momentum + grad
+    rounded = (grad + MOMENTUM_COEF * new_momentum).astype(jnp.bfloat16)
+    chunks = jnp.pad(rounded, ((0, 0), (0, 0), (0, group * width - columns)))
+    chunks = chunks.reshape(matrices, slot_rows, group, width).transpose(0, 2, 1, 3)
+    chunks = chunks.reshape(holders, slot_rows, width)
+
+    chosen = lax.axis_index("dp") // group
+    own_lengths = lax.dynamic_index_in_dim(lengths, chosen, 0, keepdims=False)
+    own_offsets = jnp.cumsum(own_lengths) - own_lengths
+    within = jnp.arange(slot_rows, dtype=jnp.int32)[None, :]
+    row = own_offsets[:, None] + within
+    row = (row + lax.rem(lax.axis_index("ep"), 2) * (H // 2)) % H
+    target = jnp.where(within < own_lengths[:, None], row, -1).reshape(-1)
+
+    held = spread(chunks).reshape(2, holders * slot_rows, width)
+    matrix, parts = local_gram(target[None, :], held)
+    blocks = reduce_parts(parts.reshape(peers, -1, parts.shape[1]), group)
+    ortho = apply_chain(target[:, None], blocks.reshape(H, -1), matrix, slot_rows)
+    back = collect(ortho.reshape(holders, slot_rows, width))
+    back = back.reshape(matrices, group, slot_rows, width).transpose(0, 2, 1, 3)
+    back = back.reshape(matrices, slot_rows, group * width)[:, :, :columns]
+    return (new_momentum, back.astype(jnp.float32) * math.sqrt(max(H, D)))
+
+
+def can_split(holders, shards, matrices, slot_rows, columns):
+    if holders % matrices or shards % 2 or slot_rows % 16:
+        return False
+    group = holders // matrices
+    if group * chunk_width(columns, group) * 3 > columns * 4:
+        return False
+    return H % (BLOCKS * LANES) == 0 and H // 2 % (group * (shards // 2) * 16) == 0
+
+
 def solution(mesh):
-    return jax.shard_map(
-        body,
-        mesh=mesh,
-        in_specs=(P(None, "dp", "ep"), P(None, "dp", "ep"), P()),
-        out_specs=(P(None, "dp", "ep"), P(None, "dp", "ep")),
-        check_vma=False,
-    )
+    def run(grad, momentum, lengths):
+        matrices, slots, columns = grad.shape
+        holders, shards = mesh.shape["dp"], mesh.shape["ep"]
+        fits = can_split(holders, shards, matrices, slots // holders, columns // shards)
+        return jax.shard_map(
+            split_body if fits else gathered_body,
+            mesh=mesh,
+            in_specs=(P(None, "dp", "ep"), P(None, "dp", "ep"), P()),
+            out_specs=(P(None, "dp", "ep"), P(None, "dp", "ep")),
+            check_vma=False,
+        )(grad, momentum, lengths)
+
+    return run

time: 357 us -> 94.7 us (0.27)
  waiting for transfers between devices: 277 us -> 0 us
  Pallas kernels: 0 us -> 80.7 us
  matrix products: 33.9 us -> 0 us
  between operations: 14.6 us -> 0.74 us
  local copies, waits for them, and re-layouts: 16.3 us -> 5.74 us
  other arithmetic: 14.6 us -> 6.61 us
    all_gather x2 -> x0, waiting for transfers between devices: 142 us -> none  [the longest x1 92 us: body(): portion = lax.all_gather(rounded, 'dp', axis=1, tiled=True)]
    psum x1 -> x0, waiting for transfers between devices: 135 us -> none  [from_root(): return lax.psum(block, axis)]
    pallas_call x0 -> x5, Pallas kernels: none -> 80.7 us  [the longest x1 26.1 us: reduce_parts(): pl.pallas_call(functools.partial(reduce_kernel, group, peers), out_shape=...]
    dot_general x4 -> x0, matrix products: 33.9 us -> none  [the longest x1 15.1 us: body(): gram_full = jnp.dot(portion, portion.T, preferred_element_type=jnp.float32)]
    scatter x1 -> x0, local copies, waits for them, and re-layouts: 9.57 us -> none  [body(): jnp.zeros((H, columns), jnp.bfloat16).at[target].set(incoming, mode='drop')]
    gather x2 -> x0, local copies, waits for them, and re-layouts: 4.17 us -> none  [body(): jnp.take(owned_ortho, jnp.where(is_valid, own_offset + positions, 0), axi...]
  transfers between devices with their start and end apart: 3 -> 0, of which waited for: 3 -> 0; matrix products, arithmetic and copies ran while one was open for 3% -> 0% of each run, Pallas kernels for 0% -> 0%
where the time goes in v1:
time: 94.7 us; the launch traced here: 93.8 us
  Pallas kernels  80.7 us (85%)
  other arithmetic  6.61 us (7%)
  local copies, waits for them, and re-layouts  5.74 us (6%)
    pallas_call x1, Pallas kernels, reduce_parts(): pl.pallas_call(functools.partial(reduce_kernel, group, peers), out_shape=...  26.1 us
    pallas_call x1, Pallas kernels, spread(): pl.pallas_call(functools.partial(spread_kernel, holders), out_shape=jax.S...  22.7 us
    pallas_call x1, Pallas kernels, collect(): pl.pallas_call(functools.partial(collect_kernel, holders), out_shape=jax....  19.6 us
    pallas_call x1, Pallas kernels, apply_chain(): pl.pallas_call(functools.partial(chain_kernel, slot_rows), out_shape=jax....  8.58 us
    pallas_call x1, Pallas kernels, local_gram(): pl.pallas_call(gram_kernel, out_shape=(jax.ShapeDtypeStruct((H, width), j...  3.67 us
    convert_element_type x1, other arithmetic, split_body(): rounded = (grad + MOMENTUM_COEF * new_momentum).astype(jnp.bfloat16)  3.07 us
    unnamed x4, local copies, waits for them, and re-layouts  2.28 us

profile of v1, /device:TPU:0, one launch (start us, length us, event | category | flops | bytes accessed | tf_op | source)
XLA Modules:
  0.0 93.8 jit_solution(8515415034999303800)
XLA Ops:
  0.6 0.7 fusion.4
  1.3 0.2 reduce-window.8
  1.5 0.7 bitcast_subtract_fusion
  2.2 0.1 add_add_fusion
  2.3 0.1 add.96
  2.4 0.1 iota_compare_fusion
  2.4 0.1 lt.57
  2.6 3.1 %add_convert_fusion = (bf16[2,192,896]{2,1,0:T(8,128)(2,1)S(1)}, f32[2,192,896]{2,1,0:T(8,128)}) fusion(f32[2,192,896]{2,1,0:T(8,128)} %param.3, f32[2,192,896]{2,1,0:T(8,128)} %param.4), kind=kLoop, calls=%fused_computation.1 | loop fusion | flops 1720320 | bytes 4816896 | tf_op jit(solution)/shard_map/convert_element_type | solution.py:458
  5.6 0.1 fusion.7
  5.7 0.9 pad_maximum_fusion
  6.6 22.7 %spread.1 = bf16[2,8,192,256]{3,2,1,0:T(8,128)(2,1)} custom-call(bf16[8,192,256]{2,1,0:T(8,128)(2,1)} %bitcast.22), custom_call_target="tpu_custom_call" | custom-call | tf_op jit(solution)/shard_map/spread/pallas_call | solution.py:164
  29.4 0.0 copy-start
  29.4 1.4 %copy-done = bf16[2,8,192,256]{3,2,1,0:T(8,128)(2,1)S(1)} copy-done((bf16[2,8,192,256]{3,2,1,0:T(8,128)(2,1)S(1)}, bf16[2,8,192,256]{3,2,1,0:T(8,128)(2,1)}, u32[]{:S(2)}) %copy-start) | copy-done | bytes 1572888
  30.8 3.7 %local_gram.1 = (bf16[1024,256]{1,0:T(8,128)(2,1)S(1)}, bf16[512,640]{1,0:T(8,128)(2,1)S(1)}) custom-call(s32[1,1536]{1,0:T(1,128)S(1)} %fusion.2.target_ref, bf16[2,1536,256]{2,1,0:T(8,128)(2,1)S(1)} %bitcast.17), custom_call_target="tpu_custom_call" | custom-call | tf_op jit(solution)/shard_map/local_gram/pallas_call | solution.py:350
  34.5 26.1 %reduce_parts.1 = bf16[2,8,64,640]{3,2,1,0:T(8,128)(2,1)S(1)} custom-call(bf16[8,64,640]{2,1,0:T(8,128)(2,1)S(1)} %bitcast.20), custom_call_target="tpu_custom_call" | custom-call | tf_op jit(solution)/shard_map/reduce_parts/pallas_call | solution.py:295
  60.6 0.6 add.99
  61.2 0.7 lt.59
  61.9 0.4 fusion.1.target_ref
  62.3 8.6 %apply_chain.1 = bf16[1536,256]{1,0:T(8,128)(2,1)S(1)} custom-call(s32[1536,1]{1,0:T(8,128)S(1)} %fusion.1.target_ref, bf16[1024,640]{1,0:T(8,128)(2,1)S(1)} %bitcast.18, bf16[1024,256]{1,0:T(8,128)(2,1)S(1)} %get-tuple-element.5.matrix_ref), custom_call_target="tpu_custom_call" | custom-call | tf_op jit(solution)/shard_map/apply_chain/pallas_call | solution.py:434
  70.9 0.0 copy-start.1
  70.9 0.9 copy-done.1
  71.7 19.6 %collect.1 = bf16[8,192,256]{2,1,0:T(8,128)(2,1)} custom-call(bf16[8,192,256]{2,1,0:T(8,128)(2,1)} %bitcast.19), custom_call_target="tpu_custom_call" | custom-call | tf_op jit(solution)/shard_map/collect/pallas_call | solution.py:201
  91.4 1.2 %copy.11 = bf16[2,4,24,8,256]{4,3,1,2,0:T(8,128)(2,1)S(1)} copy(bf16[2,4,24,8,256]{4,3,2,1,0:T(8,128)(2,1)} %bitcast.21) | data formatting | bytes 1572864 | tf_op jit(solution)/shard_map/reshape | solution.py:477
  92.6 1.2 %convert_multiply_fusion = f32[2,192,896]{2,1,0:T(8,128)} fusion(bf16[2,192,1024]{2,1,0:T(8,128)(2,1)S(1)} %bitcast.23), kind=kLoop, calls=%fused_computation | loop fusion | flops 688128 | bytes 2064384 | tf_op jit(solution)/shard_map/mul | solution.py:478
  (1 shorter events, 0.0 us)
Async XLA Ops:
  29.4 1.4 %copy-start = (bf16[2,8,192,256]{3,2,1,0:T(8,128)(2,1)S(1)}, bf16[2,8,192,256]{3,2,1,0:T(8,128)(2,1)}, u32[]{:S(2)}) copy-start(bf16[2,8,192,256]{3,2,1,0:T(8,128)(2,1)} %spread.1) | copy-start | bytes 4718596
  70.9 0.9 copy-start.1

commit v2 on v0

--- a/solution.py
+++ b/solution.py
@@ -1,8 +1,11 @@
+import functools
 import math
 
 import jax
 import jax.numpy as jnp
 from jax import lax
+from jax.experimental import pallas as pl
+from jax.experimental.pallas import tpu as pltpu
 from jax.sharding import PartitionSpec as P
 
 H = 1024
@@ -15,6 +18,12 @@
 FIRST_CUBE = -2.5
 SECOND_LIN = 1.5
 SECOND_CUBE = -0.5
+
+LANES = 128
+BLOCKS = 8
+KEPT = BLOCKS // 2 + 1
+MESH = pl.DeviceIdType.MESH
+VMEM_LIMIT = 48 * 1024 * 1024
 
 
 def from_root(block, axis, owner):
@@ -38,7 +47,7 @@
     return (SECOND_LIN * first_iter.astype(jnp.float32) + SECOND_CUBE * third).astype(jnp.bfloat16)
 
 
-def body(grad, momentum, lengths):
+def gathered_body(grad, momentum, lengths):
     matrices = grad.shape[0]
     slot_rows = grad.shape[1]
     columns = grad.shape[2]
@@ -84,11 +93,460 @@
     return (new_momentum, jnp.stack(results))
 
 
+def other_core(ep):
+    return ep + 1 - 2 * lax.rem(ep, 2)
+
+
+def rows_at(index, count):
+    return pl.ds(pl.multiple_of(index * count, count), count)
+
+
+def step_kernel(
+    holders,
+    shards,
+    lengths_ref,
+    grad_ref,
+    momentum_ref,
+    back_ref,
+    rounded,
+    held,
+    both,
+    parts,
+    terms,
+    reduced,
+    gram,
+    first,
+    applied,
+    slots,
+    chunk_sems,
+    core_sems,
+    term_sems,
+    block_sems,
+    half_sems,
+    slot_sems,
+    local,
+):
+    matrices, slot_rows, columns = grad_ref.shape
+    group = holders // matrices
+    chips = shards // 2
+    peers = group * chips
+    width = held.shape[2]
+    narrow = columns - (group - 1) * width
+    height = both.shape[0]
+    block = height // BLOCKS
+    part_rows = height // 2 // peers
+    span = KEPT * block
+
+    dp, ep = lax.axis_index("dp"), lax.axis_index("ep")
+    core = lax.rem(ep, 2)
+    mine = dp // group
+    place = lax.rem(dp, group)
+    base = dp - place
+    sibling = (dp, other_core(ep))
+
+    def chunk_of(index, core):
+        return lax.rem(index + core, group)
+
+    def with_width(chunk, use):
+        @pl.when(chunk < group - 1)
+        def _():
+            use(width)
+
+        @pl.when(chunk == group - 1)
+        def _():
+            use(narrow)
+
+    own_chunk = chunk_of(place, core)
+    sibling_chunk = chunk_of(place, 1 - core)
+
+    partners = [(lax.rem(dp + r, holders), ep) for r in range(1, holders)] + [sibling]
+    for chip in range(1, chips):
+        other = lax.rem(ep // 2 + chip, chips) * 2 + core
+        partners += [(base + k, other) for k in range(group)]
+
+    if narrow < width:
+        held[:, :, narrow:] = jnp.zeros((2, held.shape[1], width - narrow), held.dtype)
+    barrier = pltpu.get_barrier_semaphore()
+    for partner in partners:
+        pl.semaphore_signal(barrier, inc=1, device_id=partner, device_id_type=MESH)
+
+    def round_rows(j):
+        momentum = MOMENTUM_COEF * momentum_ref[j] + grad_ref[j]
+        rounded[j] = (grad_ref[j] + MOMENTUM_COEF * momentum).astype(rounded.dtype)
+
+    def chunk_copy(to, r, w):
+        start = pl.multiple_of(chunk_of(lax.rem(to, group), core) * width, LANES)
+        return pltpu.make_async_remote_copy(
+            src_ref=rounded.at[to // group, :, pl.ds(start, w)],
+            dst_ref=held.at[0, rows_at(dp, slot_rows), pl.ds(0, w)],
+            send_sem=chunk_sems.at[0, r],
+            recv_sem=chunk_sems.at[1, r],
+            device_id=(to, ep),
+            device_id_type=MESH,
+        )
+
+    def core_copy(source, r, w):
+        return pltpu.make_async_remote_copy(
+            src_ref=held.at[0, rows_at(source, slot_rows), pl.ds(0, w)],
+            dst_ref=held.at[1, rows_at(source, slot_rows), pl.ds(0, w)],
+            send_sem=core_sems.at[0, r],
+            recv_sem=core_sems.at[1, r],
+            device_id=sibling,
+            device_id_type=MESH,
+        )
+
+    round_rows(lax.rem(mine + 1, matrices))
+    pl.semaphore_wait(barrier, len(partners))
+    order = []
+    for t in range(1, matrices + 1):
+        if t > 1:
+            round_rows(lax.rem(mine + t, matrices))
+        for k in range(group):
+            if t == matrices and k == 0:
+                continue
+            order.append((t % matrices) * group + k)
+            to = lax.rem(mine + t, matrices) * group + lax.rem(place + k, group)
+            r = order[-1]
+            chunk = chunk_of(lax.rem(to, group), core)
+            with_width(chunk, lambda w, to=to, r=r: chunk_copy(to, r, w).start())
+
+    def own_move(w):
+        start = pl.multiple_of(own_chunk * width, LANES)
+        move = pltpu.make_async_copy(
+            rounded.at[mine, :, pl.ds(start, w)],
+            held.at[0, rows_at(dp, slot_rows), pl.ds(0, w)],
+            local,
+        )
+        move.start()
+        move.wait()
+
+    with_width(own_chunk, own_move)
+    with_width(own_chunk, lambda w: core_copy(dp, 0, w).start())
+
+    def source_of(r):
+        t, k = r // group, r % group
+        half = lax.rem(mine + matrices - t, matrices)
+        return half * group + lax.rem(place + group - k, group)
+
+    arrivals = [r for r in order if r < group] + [r for r in order if r >= group]
+    for r in arrivals:
+
+        def pass_on(w, r=r):
+            chunk_copy(dp, r, w).wait_recv()
+            core_copy(source_of(r), r, w).start()
+
+        with_width(own_chunk, pass_on)
+    for r in [0] + arrivals:
+        with_width(sibling_chunk, lambda w, r=r: core_copy(dp, r, w).wait_recv())
+
+    total_slots = holders * slot_rows
+    slot = lax.broadcasted_iota(jnp.int32, (1, total_slots), 1)
+    target = jnp.full((1, total_slots), -1, jnp.int32)
+    offset = core * (height // 2)
+    for d in range(holders):
+        live = lengths_ref[mine, d]
+        inside = jnp.logical_and(slot >= d * slot_rows, slot < d * slot_rows + live)
+        row = slot - d * slot_rows + offset
+        target = jnp.where(inside, jnp.where(row >= height, row - height, row), target)
+        offset = offset + live
+
+    tile = 256
+
+    def pack(step, carry):
+        start = pl.multiple_of(step * tile, tile)
+        rows = lax.broadcasted_iota(jnp.int32, (tile, total_slots), 0) + start
+        chosen = jnp.where(rows == target, 1.0, 0.0).astype(jnp.bfloat16)
+        for which in range(2):
+            packed = jnp.dot(chosen, held[which], preferred_element_type=jnp.float32)
+            both[pl.ds(start, tile), which * width : (which + 1) * width] = packed.astype(
+                jnp.bfloat16
+            )
+        return carry
+
+    lax.fori_loop(0, height // tile, pack, 0)
+
+    me = place * chips + ep // 2
+
+    def device(index):
+        return (base + index // chips, lax.rem(index, chips) * 2 + core)
+
+    def term_copy(to, r):
+        return pltpu.make_async_remote_copy(
+            src_ref=parts.at[rows_at(to, part_rows)],
+            dst_ref=terms.at[r],
+            send_sem=term_sems.at[0, r],
+            recv_sem=term_sems.at[1, r],
+            device_id=device(to),
+            device_id_type=MESH,
+        )
+
+    def multiply(step, carry):
+        start = pl.multiple_of(step * block, block)
+        part = lax.dot_general(
+            both[pl.ds(start, block), :],
+            both[pl.ds(start, span), :],
+            (((1,), (1,)), ((), ())),
+            preferred_element_type=jnp.float32,
+        )
+        parts[pl.ds(start, block), :] = part.astype(jnp.bfloat16)
+        return carry
+
+    lax.fori_loop(0, BLOCKS // 2, multiply, 0)
+    for r in range(1, peers):
+        term_copy(lax.rem(me + r, peers), r).start()
+    total = parts[rows_at(me, part_rows), :].astype(jnp.float32)
+    for r in range(1, peers):
+        term_copy(me, r).wait_recv()
+        total = total + terms[r].astype(jnp.float32)
+    reduced[...] = total.astype(reduced.dtype)
+
+    def blocks_at(index, half):
+        row = half * (height // 2) + index * part_rows
+        column = pl.multiple_of(row // block * block, block)
+        return gram.at[pl.ds(pl.multiple_of(row, part_rows), part_rows), pl.ds(column, span)]
+
+    def block_copy(to, r):
+        return pltpu.make_async_remote_copy(
+            src_ref=reduced,
+            dst_ref=blocks_at(me, 0),
+            send_sem=block_sems.at[0, r],
+            recv_sem=block_sems.at[1, r],
+            device_id=device(to),
+            device_id_type=MESH,
+        )
+
+    def half_copy(source, r):
+        return pltpu.make_async_remote_copy(
+            src_ref=reduced if r == 0 else blocks_at(source, 0),
+            dst_ref=blocks_at(source, 1),
+            send_sem=half_sems.at[0, r],
+            recv_sem=half_sems.at[1, r],
+            device_id=sibling,
+            device_id_type=MESH,
+        )
+
+    for r in range(1, peers):
+        block_copy(lax.rem(me + r, peers), r).start()
+    half_copy(me, 0).start()
+    own = pltpu.make_async_copy(reduced, blocks_at(me, 0), local)
+    own.start()
+    for r in range(1, peers):
+        block_copy(me, r).wait_recv()
+        half_copy(lax.rem(me + peers - r, peers), r).start()
+    own.wait()
+
+    squares = jnp.zeros((8, LANES), jnp.float32)
+    for i in range(BLOCKS):
+        if i == BLOCKS // 2:
+            for r in range(peers):
+                half_copy(me, r).wait_recv()
+        for k in range(KEPT):
+            j = (i + k) % BLOCKS
+            piece = gram[pl.ds(i * block, block), pl.ds((i + k) * block, block)]
+            if i + k >= BLOCKS:
+                gram[pl.ds(i * block, block), pl.ds(j * block, block)] = piece
+            wide = piece.astype(jnp.float32)
+            twice = 0 < k < BLOCKS - KEPT + 1
+            if twice:
+                gram[pl.ds(j * block, block), pl.ds(i * block, block)] = wide.T.astype(jnp.bfloat16)
+            square = (wide * wide).reshape(-1, 8, block).sum(axis=0)
+            for lane in range(block // LANES):
+                squares = squares + (2.0 if twice else 1.0) * square[
+                    :, lane * LANES : (lane + 1) * LANES
+                ]
+    scale_sq = lax.rsqrt(jnp.sum(squares, keepdims=True) + EPSILON)
+    factor = jnp.sqrt(scale_sq)
+
+    def product(start, right):
+        return scale_sq * jnp.dot(
+            gram[pl.ds(start, tile), :height], right, preferred_element_type=jnp.float32
+        )
+
+    def each(step):
+        def run(index, carry):
+            step(pl.multiple_of(index * tile, tile))
+            return carry
+
+        lax.fori_loop(0, height // tile, run, 0)
+
+    def one(start):
+        rows = both[pl.ds(start, tile), :width].astype(jnp.float32)
+        value = factor * (FIRST_LIN * rows + FIRST_CUBE * product(start, both[:, :width]))
+        first[pl.ds(start, tile), :] = value.astype(jnp.bfloat16)
+
+    def two(start):
+        rows = first[pl.ds(start, tile), :].astype(jnp.float32)
+        value = FIRST_LIN * rows + FIRST_CUBE * product(start, first[...])
+        applied[0, pl.ds(start, tile), :] = value.astype(jnp.bfloat16)
+
+    def three(start):
+        value = product(start, applied[0])
+        applied[1, pl.ds(start, tile), :] = value.astype(jnp.bfloat16)
+
+    def four(start):
+        rows = applied[1, pl.ds(start, tile), :].astype(jnp.float32)
+        third = FIRST_LIN * rows + FIRST_CUBE * product(start, applied[1])
+        rows = first[pl.ds(start, tile), :].astype(jnp.float32)
+        value = SECOND_LIN * rows + SECOND_CUBE * third
+        applied[0, pl.ds(start, tile), :] = value.astype(jnp.bfloat16)
+
+    for step in (one, two, three, four):
+        each(step)
+
+    def slot_copy(to, r, w):
+        start = pl.multiple_of(own_chunk * width, LANES)
+        return pltpu.make_async_remote_copy(
+            src_ref=slots.at[rows_at(to, slot_rows), pl.ds(0, w)],
+            dst_ref=back_ref.at[mine, :, pl.ds(start, w)],
+            send_sem=slot_sems.at[0, r],
+            recv_sem=slot_sems.at[1, r],
+            device_id=(to, ep),
+            device_id_type=MESH,
+        )
+
+    def incoming(r, w):
+        source = source_of(r)
+        start = pl.multiple_of(chunk_of(lax.rem(source, group), core) * width, LANES)
+        return pltpu.make_async_remote_copy(
+            src_ref=slots.at[rows_at(source, slot_rows), pl.ds(0, w)],
+            dst_ref=back_ref.at[source // group, :, pl.ds(start, w)],
+            send_sem=slot_sems.at[0, r],
+            recv_sem=slot_sems.at[1, r],
+            device_id=(source, ep),
+            device_id_type=MESH,
+        )
+
+    def lay_out(to):
+        start = core * (height // 2)
+        live = lengths_ref[mine, to]
+        for d in range(holders):
+            start = start + jnp.where(d < to, lengths_ref[mine, d], 0)
+        slot = lax.broadcasted_iota(jnp.int32, (slot_rows, height), 0)
+        column = lax.broadcasted_iota(jnp.int32, (slot_rows, height), 1)
+        row = slot + start
+        row = jnp.where(row >= height, row - height, row)
+        row = jnp.where(row >= height, row - height, row)
+        chosen = jnp.where(jnp.logical_and(row == column, slot < live), 1.0, 0.0)
+        rows = jnp.dot(
+            chosen.astype(jnp.bfloat16), applied[0], preferred_element_type=jnp.float32
+        )
+        slots[rows_at(to, slot_rows), :] = rows.astype(jnp.bfloat16)
+
+    def target_of(r):
+        t, k = r // group, r % group
+        return lax.rem(mine + t, matrices) * group + lax.rem(place + k, group)
+
+    for r in order:
+        to = target_of(r)
+        lay_out(to)
+        with_width(own_chunk, lambda w, to=to, r=r: slot_copy(to, r, w).start())
+    lay_out(dp)
+
+    def keep(w):
+        start = pl.multiple_of(own_chunk * width, LANES)
+        move = pltpu.make_async_copy(
+            slots.at[rows_at(dp, slot_rows), pl.ds(0, w)],
+            back_ref.at[mine, :, pl.ds(start, w)],
+            local,
+        )
+        move.start()
+        move.wait()
+
+    with_width(own_chunk, keep)
+
+    for r in order:
+        to = target_of(r)
+        chunk = chunk_of(lax.rem(to, group), core)
+        with_width(chunk, lambda w, to=to, r=r: chunk_copy(to, r, w).wait_send())
+    for r in [0] + order:
+        with_width(own_chunk, lambda w, r=r: core_copy(dp, r, w).wait_send())
+    for r in range(1, peers):
+        term_copy(me, r).wait_send()
+        block_copy(me, r).wait_send()
+    for r in range(peers):
+        half_copy(me, r).wait_send()
+    for r in order:
+        with_width(own_chunk, lambda w, r=r: slot_copy(dp, r, w).wait_send())
+        chunk = chunk_of(lax.rem(source_of(r), group), core)
+        with_width(chunk, lambda w, r=r: incoming(r, w).wait_recv())
+
+
+def orthogonalize(grad, momentum, lengths):
+    matrices, slot_rows, columns = grad.shape
+    holders, shards = lax.axis_size("dp"), lax.axis_size("ep")
+    group = holders // matrices
+    peers = group * (shards // 2)
+    width = chunk_width(columns, group)
+    block = H // BLOCKS
+    part = (H // 2 // peers, KEPT * block)
+    held = (2, holders * slot_rows, width)
+    dma = pltpu.SemaphoreType.DMA
+    vmem = pl.BlockSpec(memory_space=pltpu.VMEM)
+
+    def buffer(*shape):
+        return pltpu.VMEM(shape, jnp.bfloat16)
+
+    return pl.pallas_call(
+        functools.partial(step_kernel, holders, shards),
+        out_shape=jax.ShapeDtypeStruct(grad.shape, jnp.bfloat16),
+        in_specs=[pl.BlockSpec(memory_space=pltpu.SMEM), vmem, vmem],
+        out_specs=pl.BlockSpec(memory_space=pl.ANY),
+        scratch_shapes=[
+            buffer(*grad.shape),
+            buffer(*held),
+            buffer(H, 2 * width),
+            buffer(H // 2, KEPT * block),
+            buffer(peers, *part),
+            buffer(*part),
+            buffer(H, H + (KEPT - 1) * block),
+            buffer(H, width),
+            buffer(2, H, width),
+            buffer(holders * slot_rows, width),
+            dma((2, holders)),
+            dma((2, holders)),
+            dma((2, peers)),
+            dma((2, peers)),
+            dma((2, peers)),
+            dma((2, holders)),
+            dma,
+        ],
+        compiler_params=pltpu.CompilerParams(
+            collective_id=0, has_side_effects=True, vmem_limit_bytes=VMEM_LIMIT
+        ),
+        name="orthogonalize",
+    )(lengths, grad, momentum)
+
+
+def chunk_width(columns, group):
+    return -(-columns // (group * LANES)) * LANES
+
+
+def split_body(grad, momentum, lengths):
+    new_momentum = MOMENTUM_COEF * momentum + grad
+    back = orthogonalize(grad, momentum, lengths)
+    return (new_momentum, back.astype(jnp.float32) * math.sqrt(max(H, D)))
+
+
+def can_split(holders, shards, matrices, slot_rows, columns):
+    if holders % matrices or shards % 2 or slot_rows % 16:
+        return False
+    group = holders // matrices
+    if group * chunk_width(columns, group) * 3 > columns * 4:
+        return False
+    return H % (BLOCKS * LANES) == 0 and H // 2 % (group * (shards // 2) * 16) == 0
+
+
 def solution(mesh):
-    return jax.shard_map(
-        body,
-        mesh=mesh,
-        in_specs=(P(None, "dp", "ep"), P(None, "dp", "ep"), P()),
-        out_specs=(P(None, "dp", "ep"), P(None, "dp", "ep")),
-        check_vma=False,
-    )
+    def run(grad, momentum, lengths):
+        matrices, slots, columns = grad.shape
+        holders, shards = mesh.shape["dp"], mesh.shape["ep"]
+        fits = can_split(holders, shards, matrices, slots // holders, columns // shards)
+        return jax.shard_map(
+            split_body if fits else gathered_body,
+            mesh=mesh,
+            in_specs=(P(None, "dp", "ep"), P(None, "dp", "ep"), P()),
+            out_specs=(P(None, "dp", "ep"), P(None, "dp", "ep")),
+            check_vma=False,
+        )(grad, momentum, lengths)
+
+    return run

time: 357 us -> 79.5 us (0.22)
  waiting for transfers between devices: 277 us -> 0 us
  Pallas kernels: 0 us -> 73.5 us
  matrix products: 33.9 us -> 0 us
  between operations: 14.6 us -> 0.65 us
  local copies, waits for them, and re-layouts: 16.3 us -> 3.35 us
  other arithmetic: 14.6 us -> 1.8 us
    all_gather x2 -> x0, waiting for transfers between devices: 142 us -> none  [the longest x1 92 us: body(): portion = lax.all_gather(rounded, 'dp', axis=1, tiled=True)]
    psum x1 -> x0, waiting for transfers between devices: 135 us -> none  [from_root(): return lax.psum(block, axis)]
    pallas_call x0 -> x1, Pallas kernels: none -> 73.5 us  [orthogonalize(): pl.pallas_call(functools.partial(step_kernel, holders, shards), out_shape...]
    dot_general x4 -> x0, matrix products: 33.9 us -> none  [the longest x1 15.1 us: body(): gram_full = jnp.dot(portion, portion.T, preferred_element_type=jnp.float32)]
    scatter x1 -> x0, local copies, waits for them, and re-layouts: 9.57 us -> none  [body(): jnp.zeros((H, columns), jnp.bfloat16).at[target].set(incoming, mode='drop')]
    convert_element_type x2 -> x0, other arithmetic: 6.19 us -> none  [the longest x1 3.29 us: body(): rounded = (grad + MOMENTUM_COEF * new_momentum).astype(jnp.bfloat16)]
    gather x2 -> x0, local copies, waits for them, and re-layouts: 4.17 us -> none  [body(): jnp.take(owned_ortho, jnp.where(is_valid, own_offset + positions, 0), axi...]
  transfers between devices with their start and end apart: 3 -> 0, of which waited for: 3 -> 0; matrix products, arithmetic and copies ran while one was open for 3% -> 0% of each run, Pallas kernels for 0% -> 0%
where the time goes in v2:
time: 79.5 us; the launch traced here: 79.3 us
  Pallas kernels  73.5 us (92%)
  local copies, waits for them, and re-layouts  3.35 us (4%)
  other arithmetic  1.8 us (2%)
    pallas_call x1, Pallas kernels, orthogonalize(): pl.pallas_call(functools.partial(step_kernel, holders, shards), out_shape...  73.5 us
    unnamed x6, local copies, waits for them, and re-layouts  3.35 us
    mul x1, other arithmetic, split_body(): return (new_momentum, back.astype(jnp.float32) * math.sqrt(max(H, D)))  1.8 us

profile of v2, /device:TPU:0, one launch (start us, length us, event | category | flops | bytes accessed | tf_op | source)
XLA Modules:
  0.0 79.3 jit_solution(7884960682327819228)
XLA Ops:
  0.6 0.0 copy-start
  0.6 1.3 %copy-done = f32[2,192,896]{2,1,0:T(8,128)S(1)} copy-done((f32[2,192,896]{2,1,0:T(8,128)S(1)}, f32[2,192,896]{2,1,0:T(8,128)}, u32[]{:S(2)}) %copy-start) | copy-done | bytes 1376280
  2.0 0.0 copy-start.1
  2.0 1.3 %copy-done.1 = f32[2,192,896]{2,1,0:T(8,128)S(1)} copy-done((f32[2,192,896]{2,1,0:T(8,128)S(1)}, f32[2,192,896]{2,1,0:T(8,128)}, u32[]{:S(2)}) %copy-start.1) | copy-done | bytes 1376280
  3.3 0.0 copy-start.2
  3.3 0.7 copy-done.2
  4.0 73.5 %orthogonalize.1 = bf16[2,192,896]{2,1,0:T(8,128)(2,1)S(1)} custom-call(s32[2,8]{1,0:T(2,128)S(1)} %copy-done.2, f32[2,192,896]{2,1,0:T(8,128)S(1)} %copy-done, f32[2,192,896]{2,1,0:T(8,128)S(1)} %copy-done.1), custom_call_target="tpu_custom_call" | custom-call | tf_op jit(solution)/shard_map/orthogonalize/pallas_call | solution.py:489
  77.5 1.8 %convert_multiply_fusion = (f32[2,192,896]{2,1,0:T(8,128)}, f32[2,192,896]{2,1,0:T(8,128)}) fusion(bf16[2,192,896]{2,1,0:T(8,128)(2,1)S(1)} %orthogonalize.1, f32[2,192,896]{2,1,0:T(8,128)S(1)} %copy-done, f32[2,192,896]{2,1,0:T(8,128)S(1)} %copy-done.1), kind=kLoop, calls=%fused_computation | loop fusion | flops 1376256 | bytes 6193152 | tf_op jit(solution)/shard_map/mul | solution.py:527
Async XLA Ops:
  0.6 1.3 %copy-start = (f32[2,192,896]{2,1,0:T(8,128)S(1)}, f32[2,192,896]{2,1,0:T(8,128)}, u32[]{:S(2)}) copy-start(f32[2,192,896]{2,1,0:T(8,128)} %grad_ref.1) | copy-start | bytes 4128772
  2.0 1.3 %copy-start.1 = (f32[2,192,896]{2,1,0:T(8,128)S(1)}, f32[2,192,896]{2,1,0:T(8,128)}, u32[]{:S(2)}) copy-start(f32[2,192,896]{2,1,0:T(8,128)} %momentum_ref.1) | copy-start | bytes 4128772
  3.3 0.7 copy-start.2

commit v3 on v2

--- a/solution.py
+++ b/solution.py
@@ -23,7 +23,7 @@
 BLOCKS = 8
 KEPT = BLOCKS // 2 + 1
 MESH = pl.DeviceIdType.MESH
-VMEM_LIMIT = 48 * 1024 * 1024
+VMEM_LIMIT = 63 * 1024 * 1024
 
 
 def from_root(block, axis, owner):
@@ -105,11 +105,14 @@
     holders,
     shards,
     lengths_ref,
+    grad_hbm,
+    momentum_hbm,
+    back_ref,
     grad_ref,
     momentum_ref,
-    back_ref,
     rounded,
     held,
+    packed,
     both,
     parts,
     terms,
@@ -124,6 +127,7 @@
     block_sems,
     half_sems,
     slot_sems,
+    load_sems,
     local,
 ):
     matrices, slot_rows, columns = grad_ref.shape
@@ -164,6 +168,17 @@
         other = lax.rem(ep // 2 + chip, chips) * 2 + core
         partners += [(base + k, other) for k in range(group)]
 
+    def load(j):
+        return [
+            pltpu.make_async_copy(source.at[j], target.at[j], load_sems.at[which, j])
+            for which, (source, target) in enumerate(
+                [(grad_hbm, grad_ref), (momentum_hbm, momentum_ref)]
+            )
+        ]
+
+    for t in range(1, matrices + 1):
+        for copy in load(lax.rem(mine + t, matrices)):
+            copy.start()
     if narrow < width:
         held[:, :, narrow:] = jnp.zeros((2, held.shape[1], width - narrow), held.dtype)
     barrier = pltpu.get_barrier_semaphore()
@@ -171,6 +186,8 @@
         pl.semaphore_signal(barrier, inc=1, device_id=partner, device_id_type=MESH)
 
     def round_rows(j):
+        for copy in load(j):
+            copy.wait()
         momentum = MOMENTUM_COEF * momentum_ref[j] + grad_ref[j]
         rounded[j] = (grad_ref[j] + MOMENTUM_COEF * momentum).astype(rounded.dtype)
 
@@ -228,42 +245,58 @@
         half = lax.rem(mine + matrices - t, matrices)
         return half * group + lax.rem(place + group - k, group)
 
-    arrivals = [r for r in order if r < group] + [r for r in order if r >= group]
-    for r in arrivals:
-
-        def pass_on(w, r=r):
-            chunk_copy(dp, r, w).wait_recv()
-            core_copy(source_of(r), r, w).start()
-
-        with_width(own_chunk, pass_on)
-    for r in [0] + arrivals:
-        with_width(sibling_chunk, lambda w, r=r: core_copy(dp, r, w).wait_recv())
-
-    total_slots = holders * slot_rows
-    slot = lax.broadcasted_iota(jnp.int32, (1, total_slots), 1)
-    target = jnp.full((1, total_slots), -1, jnp.int32)
-    offset = core * (height // 2)
-    for d in range(holders):
-        live = lengths_ref[mine, d]
-        inside = jnp.logical_and(slot >= d * slot_rows, slot < d * slot_rows + live)
-        row = slot - d * slot_rows + offset
-        target = jnp.where(inside, jnp.where(row >= height, row - height, row), target)
-        offset = offset + live
-
-    tile = 256
-
-    def pack(step, carry):
-        start = pl.multiple_of(step * tile, tile)
-        rows = lax.broadcasted_iota(jnp.int32, (tile, total_slots), 0) + start
-        chosen = jnp.where(rows == target, 1.0, 0.0).astype(jnp.bfloat16)
-        for which in range(2):
-            packed = jnp.dot(chosen, held[which], preferred_element_type=jnp.float32)
-            both[pl.ds(start, tile), which * width : (which + 1) * width] = packed.astype(
-                jnp.bfloat16
-            )
-        return carry
-
-    lax.fori_loop(0, height // tile, pack, 0)
+    def first_row(holder):
+        row = core * (height // 2)
+        for d in range(holders):
+            row = row + jnp.where(d < holder, lengths_ref[mine, d], 0)
+        return row
+
+    tile = 512
+    half_slots = group * slot_rows
+
+    def pack(half, open_sum, close_sum):
+        slot = lax.broadcasted_iota(jnp.int32, (1, half_slots), 1)
+        target = jnp.full((1, half_slots), -1, jnp.int32)
+        for k in range(group):
+            start = first_row(half * group + k)
+            live = lengths_ref[mine, half * group + k]
+            inside = jnp.logical_and(slot >= k * slot_rows, slot < k * slot_rows + live)
+            row = slot - k * slot_rows + start
+            target = jnp.where(inside, jnp.where(row >= height, row - height, row), target)
+
+        def run(step, carry):
+            start = pl.multiple_of(step * tile, tile)
+            rows = lax.broadcasted_iota(jnp.int32, (tile, half_slots), 0) + start
+            chosen = jnp.where(rows == target, 1.0, 0.0).astype(jnp.bfloat16)
+            for which in range(2):
+                at = pl.ds(start, tile), pl.ds(which * width, width)
+                value = jnp.dot(
+                    chosen,
+                    held[which, rows_at(half, half_slots), :],
+                    preferred_element_type=jnp.float32,
+                )
+                if not open_sum:
+                    value = value + packed[at]
+                if close_sum:
+                    both[at] = value.astype(jnp.bfloat16)
+                else:
+                    packed[at] = value
+            return carry
+
+        lax.fori_loop(0, height // tile, run, 0)
+
+    for t in range(matrices):
+        arrivals = [r for r in order if r // group == t]
+        for r in arrivals:
+
+            def pass_on(w, r=r):
+                chunk_copy(dp, r, w).wait_recv()
+                core_copy(source_of(r), r, w).start()
+
+            with_width(own_chunk, pass_on)
+        for r in ([0] if t == 0 else []) + arrivals:
+            with_width(sibling_chunk, lambda w, r=r: core_copy(dp, r, w).wait_recv())
+        pack(lax.rem(mine + matrices - t, matrices), t == 0, t == matrices - 1)
 
     me = place * chips + ep // 2
 
@@ -280,8 +313,10 @@
             device_id_type=MESH,
         )
 
-    def multiply(step, carry):
-        start = pl.multiple_of(step * block, block)
+    owners = block // part_rows
+    for t in range(1, BLOCKS // 2 + 1):
+        row = lax.rem(me // owners + t, BLOCKS // 2)
+        start = pl.multiple_of(row * block, block)
         part = lax.dot_general(
             both[pl.ds(start, block), :],
             both[pl.ds(start, span), :],
@@ -289,11 +324,11 @@
             preferred_element_type=jnp.float32,
         )
         parts[pl.ds(start, block), :] = part.astype(jnp.bfloat16)
-        return carry
-
-    lax.fori_loop(0, BLOCKS // 2, multiply, 0)
-    for r in range(1, peers):
-        term_copy(lax.rem(me + r, peers), r).start()
+        for k in range(owners):
+            if t == BLOCKS // 2 and k == 0:
+                continue
+            to = row * owners + lax.rem(me + k, owners)
+            term_copy(to, lax.rem(to + peers - me, peers)).start()
     total = parts[rows_at(me, part_rows), :].astype(jnp.float32)
     for r in range(1, peers):
         term_copy(me, r).wait_recv()
@@ -348,7 +383,7 @@
             wide = piece.astype(jnp.float32)
             twice = 0 < k < BLOCKS - KEPT + 1
             if twice:
-                gram[pl.ds(j * block, block), pl.ds(i * block, block)] = wide.T.astype(jnp.bfloat16)
+                gram[pl.ds(j * block, block), pl.ds(i * block, block)] = piece.T
             square = (wide * wide).reshape(-1, 8, block).sum(axis=0)
             for lane in range(block // LANES):
                 squares = squares + (2.0 if twice else 1.0) * square[
@@ -481,7 +516,7 @@
     part = (H // 2 // peers, KEPT * block)
     held = (2, holders * slot_rows, width)
     dma = pltpu.SemaphoreType.DMA
-    vmem = pl.BlockSpec(memory_space=pltpu.VMEM)
+    hbm = pl.BlockSpec(memory_space=pl.ANY)
 
     def buffer(*shape):
         return pltpu.VMEM(shape, jnp.bfloat16)
@@ -489,11 +524,14 @@
     return pl.pallas_call(
         functools.partial(step_kernel, holders, shards),
         out_shape=jax.ShapeDtypeStruct(grad.shape, jnp.bfloat16),
-        in_specs=[pl.BlockSpec(memory_space=pltpu.SMEM), vmem, vmem],
-        out_specs=pl.BlockSpec(memory_space=pl.ANY),
+        in_specs=[pl.BlockSpec(memory_space=pltpu.SMEM), hbm, hbm],
+        out_specs=hbm,
         scratch_shapes=[
+            pltpu.VMEM(grad.shape, jnp.float32),
+            pltpu.VMEM(grad.shape, jnp.float32),
             buffer(*grad.shape),
             buffer(*held),
+            pltpu.VMEM((H, 2 * width), jnp.float32),
             buffer(H, 2 * width),
             buffer(H // 2, KEPT * block),
             buffer(peers, *part),
@@ -508,6 +546,7 @@
             dma((2, peers)),
             dma((2, peers)),
             dma((2, holders)),
+            dma((2, matrices)),
             dma,
         ],
         compiler_params=pltpu.CompilerParams(

time: 79.5 us -> 74.6 us (0.938)
  Pallas kernels: 73.5 us -> 70 us
  local copies, waits for them, and re-layouts: 3.35 us -> 0 us
  other arithmetic: 1.8 us -> 3.77 us
    pallas_call x1, Pallas kernels: 73.5 us -> 70 us  [orthogonalize(): pl.pallas_call(functools.partial(step_kernel, holders, shards), out_shape...]
    unnamed x6 -> x0, local copies, waits for them, and re-layouts: 3.35 us -> none
    mul x1, other arithmetic: 1.8 us -> 3.77 us  [split_body(): return (new_momentum, back.astype(jnp.float32) * math.sqrt(max(H, D)))]
where the time goes in v3:
time: 74.6 us; the launch traced here: 74.4 us
  Pallas kernels  70 us (94%)
  other arithmetic  3.77 us (5%)
    pallas_call x1, Pallas kernels, orthogonalize(): pl.pallas_call(functools.partial(step_kernel, holders, shards), out_shape...  70 us
    mul x1, other arithmetic, split_body(): return (new_momentum, back.astype(jnp.float32) * math.sqrt(max(H, D)))  3.77 us

profile of v3, /device:TPU:0, one launch (start us, length us, event | category | flops | bytes accessed | tf_op | source)
XLA Modules:
  0.0 74.4 jit_solution(9715920236848559631)
XLA Ops:
  0.6 70.0 %orthogonalize.1 = bf16[2,192,896]{2,1,0:T(8,128)(2,1)} custom-call(s32[2,8]{1,0:T(2,128)} %lengths_ref.1, f32[2,192,896]{2,1,0:T(8,128)} %grad_hbm.1, f32[2,192,896]{2,1,0:T(8,128)} %momentum_hbm.1), custom_call_target="tpu_custom_call" | custom-call | tf_op jit(solution)/shard_map/orthogonalize/pallas_call | solution.py:524
  70.6 3.8 %convert_multiply_fusion = (f32[2,192,896]{2,1,0:T(8,128)}, f32[2,192,896]{2,1,0:T(8,128)}) fusion(bf16[2,192,896]{2,1,0:T(8,128)(2,1)} %orthogonalize.1, f32[2,192,896]{2,1,0:T(8,128)} %grad_hbm.1, f32[2,192,896]{2,1,0:T(8,128)} %momentum_hbm.1), kind=kLoop, calls=%fused_computation | loop fusion | flops 1376256 | bytes 6193152 | tf_op jit(solution)/shard_map/mul | solution.py:566

commit v4 on v3

--- a/solution.py
+++ b/solution.py
@@ -23,7 +23,7 @@
 BLOCKS = 8
 KEPT = BLOCKS // 2 + 1
 MESH = pl.DeviceIdType.MESH
-VMEM_LIMIT = 63 * 1024 * 1024
+VMEM_LIMIT = 58 * 1024 * 1024
 
 
 def from_root(block, axis, owner):
@@ -108,6 +108,7 @@
     grad_hbm,
     momentum_hbm,
     back_ref,
+    fresh_ref,
     grad_ref,
     momentum_ref,
     rounded,
@@ -189,6 +190,7 @@
         for copy in load(j):
             copy.wait()
         momentum = MOMENTUM_COEF * momentum_ref[j] + grad_ref[j]
+        fresh_ref[j] = momentum
         rounded[j] = (grad_ref[j] + MOMENTUM_COEF * momentum).astype(rounded.dtype)
 
     def chunk_copy(to, r, w):
@@ -517,15 +519,19 @@
     held = (2, holders * slot_rows, width)
     dma = pltpu.SemaphoreType.DMA
     hbm = pl.BlockSpec(memory_space=pl.ANY)
+    vmem = pl.BlockSpec(memory_space=pltpu.VMEM)
 
     def buffer(*shape):
         return pltpu.VMEM(shape, jnp.bfloat16)
 
     return pl.pallas_call(
         functools.partial(step_kernel, holders, shards),
-        out_shape=jax.ShapeDtypeStruct(grad.shape, jnp.bfloat16),
+        out_shape=(
+            pltpu.VMEM(grad.shape, jnp.bfloat16),
+            pltpu.VMEM(grad.shape, jnp.float32),
+        ),
         in_specs=[pl.BlockSpec(memory_space=pltpu.SMEM), hbm, hbm],
-        out_specs=hbm,
+        out_specs=(vmem, vmem),
         scratch_shapes=[
             pltpu.VMEM(grad.shape, jnp.float32),
             pltpu.VMEM(grad.shape, jnp.float32),
@@ -561,8 +567,7 @@
 
 
 def split_body(grad, momentum, lengths):
-    new_momentum = MOMENTUM_COEF * momentum + grad
-    back = orthogonalize(grad, momentum, lengths)
+    back, new_momentum = orthogonalize(grad, momentum, lengths)
     return (new_momentum, back.astype(jnp.float32) * math.sqrt(max(H, D)))
 
 

time: 74.6 us -> 73 us (0.979)
  other arithmetic: 3.77 us -> 1.19 us
  local copies, waits for them, and re-layouts: 0 us -> 1.08 us
    mul x1, other arithmetic: 3.77 us -> 1.19 us  [split_body(): return (new_momentum, back.astype(jnp.float32) * math.sqrt(max(H, D)))]
    unnamed x0 -> x1, local copies, waits for them, and re-layouts: none -> 1.08 us
where the time goes in v4:
time: 73 us; the launch traced here: 72.8 us
  Pallas kernels  69.9 us (96%)
  other arithmetic  1.19 us (2%)
  local copies, waits for them, and re-layouts  1.08 us (1%)
    pallas_call x1, Pallas kernels, orthogonalize(): pl.pallas_call(functools.partial(step_kernel, holders, shards), out_shape...  69.9 us

profile of v4, /device:TPU:0, one launch (start us, length us, event | category | flops | bytes accessed | tf_op | source)
XLA Modules:
  0.0 72.8 jit_solution(10683660779291804075)
XLA Ops:
  0.6 69.9 %orthogonalize.1 = (bf16[2,192,896]{2,1,0:T(8,128)(2,1)S(1)}, f32[2,192,896]{2,1,0:T(8,128)S(1)}) custom-call(s32[2,8]{1,0:T(2,128)} %lengths_ref.1, f32[2,192,896]{2,1,0:T(8,128)} %grad_hbm.1, f32[2,192,896]{2,1,0:T(8,128)} %momentum_hbm.1), custom_call_target="tpu_custom_call" | custom-call | tf_op jit(solution)/shard_map/orthogonalize/pallas_call | solution.py:527
  70.6 1.1 %copy.6 = f32[2,192,896]{2,1,0:T(8,128)} copy(f32[2,192,896]{2,1,0:T(8,128)S(1)} %get-tuple-element.6) | data formatting | bytes 2752512
  71.6 1.2 %convert_multiply_fusion = f32[2,192,896]{2,1,0:T(8,128)} fusion(bf16[2,192,896]{2,1,0:T(8,128)(2,1)S(1)} %get-tuple-element.5), kind=kLoop, calls=%fused_computation | loop fusion | flops 688128 | bytes 2064384 | tf_op jit(solution)/shard_map/mul | solution.py:571

commit v5 on v4

--- a/solution.py
+++ b/solution.py
@@ -119,6 +119,7 @@
     terms,
     reduced,
     gram,
+    squares,
     first,
     applied,
     slots,
@@ -127,6 +128,7 @@
     term_sems,
     block_sems,
     half_sems,
+    own_sems,
     slot_sems,
     load_sems,
     local,
@@ -305,12 +307,27 @@
     def device(index):
         return (base + index // chips, lax.rem(index, chips) * 2 + core)
 
-    def term_copy(to, r):
+    split = 2 * block
+
+    def with_span(piece, of_core, use):
+        if piece == 0:
+            use(split)
+            return
+
+        @pl.when(of_core == 0)
+        def _():
+            use(span - split)
+
+        @pl.when(of_core != 0)
+        def _():
+            use(span - block - split)
+
+    def term_copy(to, r, piece, w):
         return pltpu.make_async_remote_copy(
-            src_ref=parts.at[rows_at(to, part_rows)],
-            dst_ref=terms.at[r],
-            send_sem=term_sems.at[0, r],
-            recv_sem=term_sems.at[1, r],
+            src_ref=parts.at[rows_at(to, part_rows), pl.ds(piece * split, w)],
+            dst_ref=terms.at[r, :, pl.ds(piece * split, w)],
+            send_sem=term_sems.at[0, piece, r],
+            recv_sem=term_sems.at[1, piece, r],
             device_id=device(to),
             device_id_type=MESH,
         )
@@ -330,68 +347,96 @@
             if t == BLOCKS // 2 and k == 0:
                 continue
             to = row * owners + lax.rem(me + k, owners)
-            term_copy(to, lax.rem(to + peers - me, peers)).start()
-    total = parts[rows_at(me, part_rows), :].astype(jnp.float32)
+            term_copy(to, lax.rem(to + peers - me, peers), 0, split).start()
     for r in range(1, peers):
-        term_copy(me, r).wait_recv()
-        total = total + terms[r].astype(jnp.float32)
-    reduced[...] = total.astype(reduced.dtype)
-
-    def blocks_at(index, half):
+        to = lax.rem(me + r, peers)
+        with_span(1, core, lambda w, to=to, r=r: term_copy(to, r, 1, w).start())
+
+    def blocks_at(index, half, piece, w):
         row = half * (height // 2) + index * part_rows
-        column = pl.multiple_of(row // block * block, block)
-        return gram.at[pl.ds(pl.multiple_of(row, part_rows), part_rows), pl.ds(column, span)]
-
-    def block_copy(to, r):
+        column = pl.multiple_of(row // block * block, block) + piece * split
+        return gram.at[
+            pl.ds(pl.multiple_of(row, part_rows), part_rows),
+            pl.ds(pl.multiple_of(column, block), w),
+        ]
+
+    def block_copy(to, r, piece, w):
         return pltpu.make_async_remote_copy(
-            src_ref=reduced,
-            dst_ref=blocks_at(me, 0),
-            send_sem=block_sems.at[0, r],
-            recv_sem=block_sems.at[1, r],
+            src_ref=reduced.at[:, pl.ds(piece * split, w)],
+            dst_ref=blocks_at(me, 0, piece, w),
+            send_sem=block_sems.at[0, piece, r],
+            recv_sem=block_sems.at[1, piece, r],
             device_id=device(to),
             device_id_type=MESH,
         )
 
-    def half_copy(source, r):
+    def half_copy(source, r, piece, w):
+        own = reduced.at[:, pl.ds(piece * split, w)]
         return pltpu.make_async_remote_copy(
-            src_ref=reduced if r == 0 else blocks_at(source, 0),
-            dst_ref=blocks_at(source, 1),
-            send_sem=half_sems.at[0, r],
-            recv_sem=half_sems.at[1, r],
+            src_ref=own if r == 0 else blocks_at(source, 0, piece, w),
+            dst_ref=blocks_at(source, 1, piece, w),
+            send_sem=half_sems.at[0, piece, r],
+            recv_sem=half_sems.at[1, piece, r],
             device_id=sibling,
             device_id_type=MESH,
         )
 
-    for r in range(1, peers):
-        block_copy(lax.rem(me + r, peers), r).start()
-    half_copy(me, 0).start()
-    own = pltpu.make_async_copy(reduced, blocks_at(me, 0), local)
-    own.start()
-    for r in range(1, peers):
-        block_copy(me, r).wait_recv()
-        half_copy(lax.rem(me + peers - r, peers), r).start()
-    own.wait()
-
-    squares = jnp.zeros((8, LANES), jnp.float32)
-    for i in range(BLOCKS):
-        if i == BLOCKS // 2:
-            for r in range(peers):
-                half_copy(me, r).wait_recv()
-        for k in range(KEPT):
-            j = (i + k) % BLOCKS
-            piece = gram[pl.ds(i * block, block), pl.ds((i + k) * block, block)]
-            if i + k >= BLOCKS:
-                gram[pl.ds(i * block, block), pl.ds(j * block, block)] = piece
-            wide = piece.astype(jnp.float32)
-            twice = 0 < k < BLOCKS - KEPT + 1
-            if twice:
-                gram[pl.ds(j * block, block), pl.ds(i * block, block)] = piece.T
-            square = (wide * wide).reshape(-1, 8, block).sum(axis=0)
-            for lane in range(block // LANES):
-                squares = squares + (2.0 if twice else 1.0) * square[
-                    :, lane * LANES : (lane + 1) * LANES
-                ]
-    scale_sq = lax.rsqrt(jnp.sum(squares, keepdims=True) + EPSILON)
+    def own_copy(piece, w):
+        return pltpu.make_async_copy(
+            reduced.at[:, pl.ds(piece * split, w)], blocks_at(me, 0, piece, w), own_sems.at[piece]
+        )
+
+    def reduce_piece(piece, w):
+        at = pl.ds(piece * split, w)
+        total = parts[rows_at(me, part_rows), at].astype(jnp.float32)
+        for r in range(1, peers):
+            term_copy(me, r, piece, w).wait_recv()
+            total = total + terms[r, :, at].astype(jnp.float32)
+        reduced[:, at] = total.astype(reduced.dtype)
+        for r in range(1, peers):
+            block_copy(lax.rem(me + r, peers), r, piece, w).start()
+        half_copy(me, 0, piece, w).start()
+        own_copy(piece, w).start()
+
+    def forward_piece(piece, w):
+        for r in range(1, peers):
+            block_copy(me, r, piece, w).wait_recv()
+            half_copy(lax.rem(me + peers - r, peers), r, piece, w).start()
+        own_copy(piece, w).wait()
+
+    def await_half(piece, w):
+        for r in range(peers):
+            half_copy(me, r, piece, w).wait_recv()
+
+    def assemble(half, blocks):
+        for i in range(half * BLOCKS // 2, (half + 1) * BLOCKS // 2):
+            for k in blocks:
+
+                def place(i=i, k=k):
+                    j = (i + k) % BLOCKS
+                    piece = gram[pl.ds(i * block, block), pl.ds((i + k) * block, block)]
+                    if i + k >= BLOCKS:
+                        gram[pl.ds(i * block, block), pl.ds(j * block, block)] = piece
+                    if k > 0:
+                        gram[pl.ds(j * block, block), pl.ds(i * block, block)] = piece.T
+                    wide = piece.astype(jnp.float32)
+                    square = (wide * wide).reshape(-1, 8, block).sum(axis=0)
+                    squares[...] += (2.0 if k > 0 else 1.0) * square
+
+                if k == KEPT - 1:
+                    pl.when(core == half)(place)
+                else:
+                    place()
+
+    squares[...] = jnp.zeros(squares.shape, squares.dtype)
+    for piece in range(2):
+        with_span(piece, core, functools.partial(reduce_piece, piece))
+    for piece, blocks in ((0, range(2)), (1, range(2, KEPT))):
+        with_span(piece, core, functools.partial(forward_piece, piece))
+        assemble(0, blocks)
+        with_span(piece, 1 - core, functools.partial(await_half, piece))
+        assemble(1, blocks)
+    scale_sq = lax.rsqrt(jnp.sum(squares[...], keepdims=True) + EPSILON)
     factor = jnp.sqrt(scale_sq)
 
     def product(start, right):
@@ -497,11 +542,15 @@
         with_width(chunk, lambda w, to=to, r=r: chunk_copy(to, r, w).wait_send())
     for r in [0] + order:
         with_width(own_chunk, lambda w, r=r: core_copy(dp, r, w).wait_send())
-    for r in range(1, peers):
-        term_copy(me, r).wait_send()
-        block_copy(me, r).wait_send()
-    for r in range(peers):
-        half_copy(me, r).wait_send()
+    def drain(piece, w):
+        for r in range(1, peers):
+            term_copy(me, r, piece, w).wait_send()
+            block_copy(me, r, piece, w).wait_send()
+        for r in range(peers):
+            half_copy(me, r, piece, w).wait_send()
+
+    for piece in range(2):
+        with_span(piece, core, functools.partial(drain, piece))
     for r in order:
         with_width(own_chunk, lambda w, r=r: slot_copy(dp, r, w).wait_send())
         chunk = chunk_of(lax.rem(source_of(r), group), core)
@@ -543,14 +592,16 @@
             buffer(peers, *part),
             buffer(*part),
             buffer(H, H + (KEPT - 1) * block),
+            pltpu.VMEM((8, block), jnp.float32),
             buffer(H, width),
             buffer(2, H, width),
             buffer(holders * slot_rows, width),
             dma((2, holders)),
             dma((2, holders)),
-            dma((2, peers)),
-            dma((2, peers)),
-            dma((2, peers)),
+            dma((2, 2, peers)),
+            dma((2, 2, peers)),
+            dma((2, 2, peers)),
+            dma((2,)),
             dma((2, holders)),
             dma((2, matrices)),
             dma,

time: 73 us -> 69.2 us (0.948)
  Pallas kernels: 69.9 us -> 66.2 us
    pallas_call x1, Pallas kernels: 69.9 us -> 66.2 us  [orthogonalize(): pl.pallas_call(functools.partial(step_kernel, holders, shards), out_shape...]
where the time goes in v5:
time: 69.2 us; the launch traced here: 69.1 us
  Pallas kernels  66.2 us (96%)
  other arithmetic  1.19 us (2%)
  local copies, waits for them, and re-layouts  1.08 us (2%)
    pallas_call x1, Pallas kernels, orthogonalize(): pl.pallas_call(functools.partial(step_kernel, holders, shards), out_shape...  66.2 us

profile of v5, /device:TPU:0, one launch (start us, length us, event | category | flops | bytes accessed | tf_op | source)
XLA Modules:
  0.0 69.1 jit_solution(815082662748535211)
XLA Ops:
  0.6 66.2 %orthogonalize.1 = (bf16[2,192,896]{2,1,0:T(8,128)(2,1)S(1)}, f32[2,192,896]{2,1,0:T(8,128)S(1)}) custom-call(s32[2,8]{1,0:T(2,128)} %lengths_ref.1, f32[2,192,896]{2,1,0:T(8,128)} %grad_hbm.1, f32[2,192,896]{2,1,0:T(8,128)} %momentum_hbm.1), custom_call_target="tpu_custom_call" | custom-call | tf_op jit(solution)/shard_map/orthogonalize/pallas_call | solution.py:576
  66.8 1.1 %copy.6 = f32[2,192,896]{2,1,0:T(8,128)} copy(f32[2,192,896]{2,1,0:T(8,128)S(1)} %get-tuple-element.6) | data formatting | bytes 2752512
  67.9 1.2 %convert_multiply_fusion = f32[2,192,896]{2,1,0:T(8,128)} fusion(bf16[2,192,896]{2,1,0:T(8,128)(2,1)S(1)} %get-tuple-element.5), kind=kLoop, calls=%fused_computation | loop fusion | flops 688128 | bytes 2064384 | tf_op jit(solution)/shard_map/mul | solution.py:622

commit v6 on v5

--- a/solution.py
+++ b/solution.py
@@ -360,10 +360,24 @@
             pl.ds(pl.multiple_of(column, block), w),
         ]
 
-    def block_copy(to, r, piece, w):
+    bits = [1 << b for b in range(peers.bit_length() - 1)]
+    passes = {}
+    if len(bits) > 2:
+        passes = {bit: bit + bits[(b + 1) % len(bits)] for b, bit in enumerate(bits)}
+    direct = bits + [m for m in range(1, peers) if m not in bits and m not in passes.values()]
+
+    def flip(mask):
+        other = me
+        for bit in bits:
+            if mask & bit:
+                other = other + bit * (1 - 2 * lax.rem(me // bit, 2))
+        return other
+
+    def block_copy(source, to, r, piece, w):
+        there = blocks_at(source, 0, piece, w)
         return pltpu.make_async_remote_copy(
-            src_ref=reduced.at[:, pl.ds(piece * split, w)],
-            dst_ref=blocks_at(me, 0, piece, w),
+            src_ref=reduced.at[:, pl.ds(piece * split, w)] if source is me else there,
+            dst_ref=there,
             send_sem=block_sems.at[0, piece, r],
             recv_sem=block_sems.at[1, piece, r],
             device_id=device(to),
@@ -393,15 +407,18 @@
             term_copy(me, r, piece, w).wait_recv()
             total = total + terms[r, :, at].astype(jnp.float32)
         reduced[:, at] = total.astype(reduced.dtype)
-        for r in range(1, peers):
-            block_copy(lax.rem(me + r, peers), r, piece, w).start()
+        for mask in direct:
+            block_copy(me, flip(mask), mask, piece, w).start()
         half_copy(me, 0, piece, w).start()
         own_copy(piece, w).start()
 
     def forward_piece(piece, w):
-        for r in range(1, peers):
-            block_copy(me, r, piece, w).wait_recv()
-            half_copy(lax.rem(me + peers - r, peers), r, piece, w).start()
+        for mask in direct + sorted(passes.values()):
+            source = flip(mask)
+            block_copy(me, me, mask, piece, w).wait_recv()
+            half_copy(source, mask, piece, w).start()
+            if mask in passes:
+                block_copy(source, flip(passes[mask] - mask), passes[mask], piece, w).start()
         own_copy(piece, w).wait()
 
     def await_half(piece, w):
@@ -545,7 +562,7 @@
     def drain(piece, w):
         for r in range(1, peers):
             term_copy(me, r, piece, w).wait_send()
-            block_copy(me, r, piece, w).wait_send()
+            block_copy(me, me, r, piece, w).wait_send()
         for r in range(peers):
             half_copy(me, r, piece, w).wait_send()
 
@@ -626,9 +643,12 @@
     if holders % matrices or shards % 2 or slot_rows % 16:
         return False
     group = holders // matrices
+    peers = group * (shards // 2)
+    if peers & (peers - 1):
+        return False
     if group * chunk_width(columns, group) * 3 > columns * 4:
         return False
-    return H % (BLOCKS * LANES) == 0 and H // 2 % (group * (shards // 2) * 16) == 0
+    return H % (BLOCKS * LANES) == 0 and H // 2 % (peers * 16) == 0
 
 
 def solution(mesh):

time: 69.2 us -> 70.9 us (1.025)
  Pallas kernels: 66.2 us -> 67.9 us
    pallas_call x1, Pallas kernels: 66.2 us -> 67.9 us  [orthogonalize(): pl.pallas_call(functools.partial(step_kernel, holders, shards), out_shape...]
where the time goes in v6:
time: 70.9 us; the launch traced here: 70.8 us
  Pallas kernels  67.9 us (96%)
  other arithmetic  1.19 us (2%)
  local copies, waits for them, and re-layouts  1.08 us (2%)
    pallas_call x1, Pallas kernels, orthogonalize(): pl.pallas_call(functools.partial(step_kernel, holders, shards), out_shape...  67.9 us

profile of v6, /device:TPU:0, one launch (start us, length us, event | category | flops | bytes accessed | tf_op | source)
XLA Modules:
  0.0 70.8 jit_solution(4298527824418933185)
XLA Ops:
  0.6 67.9 %orthogonalize.1 = (bf16[2,192,896]{2,1,0:T(8,128)(2,1)S(1)}, f32[2,192,896]{2,1,0:T(8,128)S(1)}) custom-call(s32[2,8]{1,0:T(2,128)} %lengths_ref.1, f32[2,192,896]{2,1,0:T(8,128)} %grad_hbm.1, f32[2,192,896]{2,1,0:T(8,128)} %momentum_hbm.1), custom_call_target="tpu_custom_call" | custom-call | tf_op jit(solution)/shard_map/orthogonalize/pallas_call | solution.py:593
  68.5 1.1 %copy.6 = f32[2,192,896]{2,1,0:T(8,128)} copy(f32[2,192,896]{2,1,0:T(8,128)S(1)} %get-tuple-element.6) | data formatting | bytes 2752512
  69.6 1.2 %convert_multiply_fusion = f32[2,192,896]{2,1,0:T(8,128)} fusion(bf16[2,192,896]{2,1,0:T(8,128)(2,1)S(1)} %get-tuple-element.5), kind=kLoop, calls=%fused_computation | loop fusion | flops 688128 | bytes 2064384 | tf_op jit(solution)/shard_map/mul | solution.py:639
